TPU v7x, 256 devices: a whole 4x4x8 slice. The times are simulated.
256 devices in a mesh: gx: 16 (over y, x_hi, core), gy: 8 (over z), ga: 2 (over x_lo).
Axes of the slice: x: 4 (x_hi: 2, x_lo: 2; x = x_hi * 2 + x_lo), y: 4, z: 8, core: 2. Of those that a mesh axis runs over, the one named last changes fastest.
Arguments:
- velocity: float32 [2, 256, 1024], P(None, 'gx', 'gy'), may hold values from -6 to 6
- density: float32 [256, 1024], P('gx', 'gy'), may hold values from 0.25 to 2
- grain_stress: float32 [6, 128, 256, 1024], P(None, 'ga', 'gx', 'gy'), may hold values from -4 to 4
- grain_angles: float32 [3, 128, 256, 1024], P(None, 'ga', 'gx', 'gy'), may hold values from -3.140625 to 3.140625
- hardness: float32 [128, 256, 1024], P('ga', 'gx', 'gy'), may hold values from 0.1 to 1
- active: int32 [2, 128, 256, 1024], P(None, 'ga', 'gx', 'gy'), may hold values from 0 to 4095
- donor_faces: int32 [2, 256, 1024], P(None, 'gx', 'gy'), may hold values 0 or 1
Outputs:
- velocity_out: float32 [2, 256, 1024], P(None, 'gx', 'gy')
- stress_out: float32 [6, 128, 256, 1024], P(None, 'ga', 'gx', 'gy')
- zone_stress: float32 [3, 256, 1024], P(None, 'gx', 'gy')
Inputs may be any that keep to these rules, and one draw needn't show every extreme that they name: Bit b of word w, for b below 12, is 1 when slip system 12 * w + b of that grain is active; higher bits are zero. `donor_faces`: 1 when the face takes its value from the zone itself, 0 when from the next zone along that direction.
All inputs are finite; a program needn't handle non-finite values. No bound on the sum of `donor_faces` on one device may be relied on, other than what follows from the above.
Results may differ from a plain program's by a relative error of at most 0.0001.
Values sent between devices are 32-bit elements; how exact they have to be, the bound alone decides.
No kernel may reach another device: no remote copies, remote signals or barrier semaphores. Data moves between devices by JAX's collectives and lax.ppermute only.
A program may use at most 128 MiB of HBM per device.

v0:
```python
import functools
import math

import jax
import jax.numpy as jnp
import numpy as np
from jax import lax
from jax.experimental import pallas as pl
from jax.experimental.pallas import tpu as pltpu
from jax.sharding import PartitionSpec as P

G = 128
ITERS = 4

time_step = 0.1
lame_first = 1.5
batch = 4
grain_block = 2 * batch
system_list = (
    ((0, 1, 1), (1, 1, -1)),
    ((0, 1, 1), (1, -1, 1)),
    ((1, 0, 1), (1, 1, -1)),
    ((1, 0, 1), (-1, 1, 1)),
    ((1, 1, 0), (1, -1, 1)),
    ((1, 1, 0), (-1, 1, 1)),
    ((0, 1, -1), (1, 1, 1)),
    ((0, 1, -1), (1, -1, -1)),
    ((1, 0, -1), (1, 1, 1)),
    ((1, 0, -1), (1, -1, 1)),
    ((1, -1, 0), (1, 1, 1)),
    ((1, -1, 0), (1, 1, -1)),
    ((1, 1, 2), (1, 1, -1)),
    ((1, 1, -2), (1, 1, 1)),
    ((1, -1, 2), (1, -1, -1)),
    ((-1, 1, 2), (-1, 1, -1)),
    ((1, 2, 1), (1, -1, 1)),
    ((1, -2, 1), (1, 1, 1)),
    ((-1, 2, 1), (1, 1, -1)),
    ((1, 2, -1), (-1, 1, 1)),
    ((2, 1, 1), (-1, 1, 1)),
    ((-2, 1, 1), (1, 1, 1)),
    ((2, -1, 1), (1, 1, -1)),
    ((2, 1, -1), (1, -1, 1)),
)
upper_pairs = [(i, j) for i in range(5) for j in range(i, 5)]
n_sums = 26


def slip_sums_table():
    table = np.zeros((n_sums, 24))
    for s, (normal, direction) in enumerate(system_list):
        q = np.outer(direction, normal) + np.outer(normal, direction)
        k = np.array([(q[0, 0] - q[1, 1]) / 2, -q[2, 2] / 2, q[1, 2], q[0, 2], q[0, 1]])
        weight = 3 if s < 12 else 1
        for e, (i, j) in enumerate(upper_pairs):
            table[e, s] = weight * k[i] * k[j] * (3 if i == j == 1 else 1)
        first = 15 if s < 12 else 20
        table[first : first + 5, s] = k
        table[25, s] = 1
    columns = np.zeros((n_sums, 24))
    for s in range(24):
        word, bit = divmod(s, 12)
        columns[:, 2 * bit + word] = table[:, s]
    return columns


def fill_table(table):
    columns = slip_sums_table()
    lane = lax.broadcasted_iota(jnp.int32, (8, 192), 1)
    own = lane % 8 == lax.broadcasted_iota(jnp.int32, (8, 192), 0)
    system = lane // 8
    for e in range(n_sums):
        entry = jnp.zeros((8, 192), jnp.float32)
        for k in range(24):
            if columns[e, k]:
                entry = jnp.where(system == k, float(columns[e, k]), entry)
        table[8 * e : 8 * e + 8] = jnp.where(own, entry, 0.0)


def fitted(function, degree, top):
    series = np.polynomial.chebyshev.Chebyshev.interpolate(function, degree, domain=[0.0, top])
    return [float(c) for c in series.convert(kind=np.polynomial.Polynomial).coef]


angle_top = 3.1416**2
sin_half = fitted(lambda t: math.sqrt(2) * np.sin(np.sqrt(t) / 2) / np.sqrt(t), 4, angle_top)
cos_half = fitted(lambda t: math.sqrt(2) * np.cos(np.sqrt(t) / 2), 4, angle_top)


def polynomial(t, coefs):
    total = coefs[-1] * t + coefs[-2]
    for c in coefs[-3::-1]:
        total = total * t + c
    return total


def sin_cos(x):
    t = x * x
    s = x * polynomial(t, sin_half)
    c = polynomial(t, cos_half)
    return s * c, 1.0 - s * s


def grain_math(stress, angles, hardness, sums, strain):
    exx, eyy, exy, trace, hydro = strain
    s1, c1 = sin_cos(angles[0])
    sq, cq = sin_cos(angles[1])
    s2, c2 = sin_cos(angles[2])
    c1c2, s1s2, c1s2, s1c2 = c1 * c2, s1 * s2, c1 * s2, s1 * c2
    r00 = c1c2 - s1s2 * cq
    r01 = -(c1s2 + s1c2 * cq)
    r02 = s1 * sq
    r10 = s1c2 + c1s2 * cq
    r11 = c1c2 * cq - s1s2
    r12 = -(c1 * sq)
    a0, b0 = r00 * exx + r10 * exy, r10 * eyy + r00 * exy
    a1, b1 = r01 * exx + r11 * exy, r11 * eyy + r01 * exy
    d00 = r00 * a0 + r10 * b0
    d11 = r01 * a1 + r11 * b1
    t00, t11 = stress[0] + d00, stress[1] + d11
    t22 = stress[2] + (trace - (d00 + d11))
    t_sum = t00 + t11
    v = [
        (t00 - t11) * 0.5,
        t_sum * (1 / math.sqrt(12)) - t22 * (2 / math.sqrt(12)),
        stress[3] + (r02 * a1 + r12 * b1),
        stress[4] + (r02 * a0 + r12 * b0),
        stress[5] + (r01 * a0 + r11 * b0),
    ]
    pressure = (t_sum + t22) * (1.0 / 3.0) + hydro
    step = 1.0 / (1.0 + sums(25))
    h0 = hardness * step * (1 / math.sqrt(2))
    h1 = h0 * (1 / math.sqrt(3))
    h2 = h0 * (1.0 / 3.0)
    bias = []
    for i in range(5):
        first, second = (h0, h1) if i == 1 else (h1, h2)
        bias.append(sums(15 + i) * first + sums(20 + i) * second)
    plain, mixed = step * (1 / 18.0), step * (math.sqrt(3) / 18.0)
    m = {}
    for e, (i, j) in enumerate(upper_pairs):
        entry = sums(e) * (mixed if (i == 1) != (j == 1) else plain)
        m[i, j] = m[j, i] = (1.0 - entry) if i == j else entry
    for _ in range(ITERS):
        fresh = []
        for i in range(5):
            off = None
            for j in range(5):
                if j != i:
                    term = m[i, j] * v[j]
                    off = term if off is None else off + term
            fresh.append((m[i, i] * v[i] + bias[i]) - off)
        v = fresh
    w = v[1] * (1 / math.sqrt(3))
    mid = pressure + w
    x = [mid + v[0], mid - v[0], pressure - 2.0 * w, v[2], v[3], v[4]]
    f0 = x[0] * r00 + x[5] * r01 + x[4] * r02
    f1 = x[5] * r00 + x[1] * r01 + x[3] * r02
    f2 = x[4] * r00 + x[3] * r01 + x[2] * r02
    g0 = x[0] * r10 + x[5] * r11 + x[4] * r12
    g1 = x[5] * r10 + x[1] * r11 + x[3] * r12
    g2 = x[4] * r10 + x[3] * r11 + x[2] * r12
    sample = (
        r00 * f0 + r01 * f1 + r02 * f2,
        r10 * g0 + r11 * g1 + r12 * g2,
        r00 * g0 + r01 * g1 + r02 * g2,
    )
    return x, sample


def bit_rows(words):
    pieces = [jnp.concatenate([w[:8], w[8:]], axis=1) for w in words]
    both = jnp.concatenate(pieces, axis=0).astype(jnp.int16)
    one, none = jnp.bfloat16(1.0), jnp.bfloat16(0.0)
    rows = [jnp.where((both & jnp.int16(1 << bit)) != 0, one, none) for bit in range(12)]
    return jnp.concatenate(rows, axis=0)


def places():
    return lax.axis_index("gx"), lax.axis_index("gy")


def sizes():
    return lax.axis_size("gx"), lax.axis_size("gy")


def whole(*shape):
    return pl.BlockSpec(shape, lambda *i: (0,) * len(shape))


def f32(*shape):
    return jax.ShapeDtypeStruct(shape, jnp.float32)


def lane_ids(rows):
    return lax.broadcasted_iota(jnp.int32, (rows, 128), 1)


def row_ids():
    return lax.broadcasted_iota(jnp.int32, (16, 128), 0)


def from_sides(got_even, got_odd, index, count):
    odd = index % 2 == 1
    after = jnp.where(odd, got_odd, got_even)
    before = jnp.where(odd, got_even, got_odd)
    return jnp.where(index == count - 1, 0.0, after), jnp.where(index == 0, 0.0, before)


def shifts_x(field, east, west):
    row = row_ids()
    return (
        jnp.where(row == 15, east, pltpu.roll(field, 15, 0)),
        jnp.where(row == 0, west, pltpu.roll(field, 1, 0)),
    )


def shifts_y(field, halo):
    lane = lane_ids(field.shape[0])
    return (
        jnp.where(lane == 127, halo, pltpu.roll(field, 127, 1)),
        jnp.where(lane == 0, halo, pltpu.roll(field, 1, 1)),
    )


def side_columns(after, before, first, last):
    lane = lane_ids(after.shape[0])
    return jnp.where(
        lane == 127,
        pltpu.roll(after, 127 - first, 1),
        jnp.where(lane == 0, pltpu.roll(before, (128 - last) % 128, 1), 0.0),
    )


def velocity_halo(counts, got):
    gx, gy = places()
    after_x, before_x = from_sides(got[0], got[1], gx, counts[0])
    after_y, before_y = from_sides(got[2], got[3], gy, counts[1])
    return after_x[0:1], before_x[15:16], side_columns(after_y, before_y, 0, 127)


def solve_kernel(
    counts, half_velocity, x_even, x_odd, y_even, y_odd, stress_in, angles_in, hardness_in, active_in,
    relaxed_out, zone_sum, rows_even, rows_odd, cols_even, cols_odd,
    relaxed, stress, angles, hardness, active, table_wide, table, sums_a, sums_b, strain, cols, sems, out_sems,
):
    blocks = hardness.shape[0] // grain_block
    gx, gy = places()

    def copies(i, kinds):
        part = pl.ds(i * grain_block, grain_block)
        every = (
            lambda: (active_in.at[:, part], active.at[:, part]),
            lambda: (stress_in.at[:, part], stress.at[:, part]),
            lambda: (angles_in.at[:, part], angles.at[:, part]),
            lambda: (hardness_in.at[part], hardness.at[part]),
        )
        return [pltpu.make_async_copy(*every[k](), sems.at[k, i]) for k in kinds]

    def out_copy(i):
        part = pl.ds(i * grain_block, grain_block)
        return pltpu.make_async_copy(relaxed.at[0:6, part], relaxed_out.at[:, part], out_sems.at[i])

    def count(group, sums):
        first = group * batch
        bits = [bit_rows([active[0, first + k], active[1, first + k]]) for k in range(batch)]
        sums[...] = jnp.dot(
            table[...], jnp.concatenate(bits, axis=1), preferred_element_type=jnp.float32
        )

    def update(group, sums):
        lane = lane_ids(8)
        for half in range(2):
            part = pl.ds(8 * half, 8)
            zone_strain = [strain[i, part] for i in range(5)]
            totals = [zone_sum[k, part] for k in range(3)]
            ends = [cols[c, part] for c in range(6)]
            for k in range(batch):
                g = group * batch + k
                lanes = slice(256 * k + 128 * half, 256 * k + 128 * half + 128)
                x, sample = grain_math(
                    [stress[c, g, part] for c in range(6)],
                    [angles[c, g, part] for c in range(3)],
                    hardness[g, part],
                    lambda e: sums[e * 8 : (e + 1) * 8, lanes],
                    zone_strain,
                )
                here = (lane == 2 * g) | (lane == 2 * g + 1)
                for c in range(6):
                    relaxed[c, g, part] = x[c]
                    ends[c] = jnp.where(here, pltpu.roll(x[c], 2 * g + 1, 1), ends[c])
                totals = [t + s for t, s in zip(totals, sample)]
            for k in range(3):
                zone_sum[k, part] = totals[k]
            for c in range(6):
                cols[c, part] = ends[c]

    for copy in copies(0, range(4)):
        copy.start()
    for copy in copies(1, range(4)):
        copy.start()
    fill_table(table_wide)
    table[...] = table_wide[...].astype(jnp.bfloat16)
    zone_sum[...] = jnp.zeros_like(zone_sum)
    cols[...] = jnp.zeros_like(cols)
    grads = []
    for k in range(2):
        u = half_velocity[k]
        east, west, halo = velocity_halo(counts, (x_even[k], x_odd[k], y_even[k], y_odd[k]))
        u_east, u_west = shifts_x(u, 0.5 * east, 0.5 * west)
        u_north, u_south = shifts_y(u, 0.5 * halo)
        grads.append((u_east - u_west, u_north - u_south))
    exx, eyy = grads[0][0], grads[1][1]
    exy = 0.5 * (grads[0][1] + grads[1][0])
    strain[0] = 2.0 * time_step * exx
    strain[1] = 2.0 * time_step * eyy
    strain[2] = 2.0 * time_step * exy
    strain[3] = 2.0 * time_step * (exx + eyy)
    strain[4] = lame_first * time_step * (exx + eyy)
    for i in range(2, blocks):
        for copy in copies(i, range(4)):
            copy.start()
    copies(0, [0])[0].wait()
    count(0, sums_a)

    def step(block, carry):
        for copy in copies(block, [1, 2, 3]):
            copy.wait()

        @pl.when(block < blocks - 1)
        def _():
            copies(block + 1, [0])[0].wait()

        group = block * 2
        count(group + 1, sums_b)
        update(group, sums_a)
        count(jnp.minimum(group + 2, blocks * 2 - 1), sums_a)
        update(group + 1, sums_b)
        out_copy(block).start()
        return carry

    lax.fori_loop(0, blocks, step, 0)

    n = relaxed.shape[1]
    flat = relaxed.reshape(7 * n * 16, 128)
    odd_x, odd_y = gx % 2 == 1, gy % 2 == 1
    for c in range(6):
        first = flat[pl.ds(c * n * 16, n, stride=16)]
        last = flat[pl.ds(c * n * 16 + 15, n, stride=16)]
        rows_even[c] = jnp.where(odd_x, first, last)
        rows_odd[c] = jnp.where(odd_x, last, first)
    low = lane_ids(16) % 2 == 0
    for c in range(3):
        one, other = cols[c], cols[c + 3]
        last = jnp.where(low, one, pltpu.roll(other, 1, 1))
        first = jnp.where(low, pltpu.roll(one, 127, 1), other)
        cols_even[c] = jnp.where(odd_y, first, last)
        cols_odd[c] = jnp.where(odd_y, last, first)
    for i in range(blocks):
        out_copy(i).wait()


def solve_grains(half_velocity, got, stress, angles, hardness, active):
    n = hardness.shape[0]
    in_hbm = pl.BlockSpec(memory_space=pltpu.HBM)
    return pl.pallas_call(
        functools.partial(solve_kernel, sizes()),
        grid=(1,),
        in_specs=[
            whole(2, 16, 128),
            *[whole(*g.shape) for g in got],
            *[in_hbm] * 4,
        ],
        out_specs=[
            in_hbm,
            whole(3, 16, 128),
            whole(6, n, 128),
            whole(6, n, 128),
            whole(3, 16, 128),
            whole(3, 16, 128),
        ],
        out_shape=[f32(6, n, 16, 128), f32(3, 16, 128), f32(6, n, 128), f32(6, n, 128)]
        + [f32(3, 16, 128)] * 2,
        scratch_shapes=[
            pltpu.VMEM((7, n, 16, 128), jnp.float32),
            pltpu.VMEM(stress.shape, jnp.float32),
            pltpu.VMEM(angles.shape, jnp.float32),
            pltpu.VMEM(hardness.shape, jnp.float32),
            pltpu.VMEM(active.shape, jnp.int32),
            pltpu.VMEM((8 * n_sums, 192), jnp.float32),
            pltpu.VMEM((8 * n_sums, 192), jnp.bfloat16),
            pltpu.VMEM((8 * n_sums, 256 * batch), jnp.float32),
            pltpu.VMEM((8 * n_sums, 256 * batch), jnp.float32),
            pltpu.VMEM((5, 16, 128), jnp.float32),
            pltpu.VMEM((6, 16, 128), jnp.float32),
            pltpu.SemaphoreType.DMA((4, n // grain_block)),
            pltpu.SemaphoreType.DMA((n // grain_block,)),
        ],
        compiler_params=pltpu.CompilerParams(vmem_limit_bytes=53 * 2**20),
        cost_estimate=pl.CostEstimate(flops=10**8, bytes_accessed=10**7, transcendentals=0),
    )(half_velocity, *got, stress, angles, hardness, active)


def zone_update(counts, velocity, fields, u_got, stress, s_got, tall, moved, velocity_out):
    gx, gy = places()
    sx_even, sx_odd, sy_even, sy_odd = s_got
    s_east, s_west = from_sides(sx_even, sx_odd, gx, counts[0])
    s_north, s_south = from_sides(sy_even, sy_odd, gy, counts[1])
    for c in range(3):
        tall[c, 0:2] = s_west[2 * c : 2 * c + 2]
        tall[c, 2:18] = stress[c]
        tall[c, 18:20] = s_east[2 * c : 2 * c + 2]
    near = [side_columns(s_north, s_south, 4 * c + 2, 4 * c + 1) for c in range(3)]
    far = [side_columns(s_north, s_south, 4 * c + 3, 4 * c) for c in range(3)]
    lane = lane_ids(16)
    sign = jnp.where(lane == 127, 0.5, -0.5)

    def x_diff(c):
        return (tall[c, 2:20] - tall[c, 0:18]) * 0.5

    def y_diff(c):
        after, before = shifts_y(tall[c, 1:19], near[c][:18])
        return (after - before) * 0.5

    def rim_x(c):
        return (near[c][2:18] - near[c][0:16]) * 0.5

    def rim_y(c):
        return (far[c][1:17] - stress[c]) * sign

    force = [x_diff(0) + y_diff(2), x_diff(2) + y_diff(1)]
    rim_force = [rim_x(0) + rim_y(2), rim_x(2) + rim_y(1)]
    field_rim = [
        side_columns(s_north[:16], s_south[:16], 13 + 2 * k, 12 + 2 * k) for k in range(3)
    ]
    sides = [velocity_halo(counts, [got[k] for got in u_got]) for k in range(2)]

    def high(k):
        return jnp.concatenate([s_west[6 + k : 7 + k], fields[k], s_east[6 + k : 7 + k]], axis=0)

    mass = time_step * high(0)
    rim = []
    for k in range(2):
        east, west, halo = sides[k]
        moved[k, 0:18] = jnp.concatenate([west, velocity[k], east], axis=0) + mass * force[k]
        rim.append(halo + time_step * field_rim[0] * rim_force[k])
    frac_x = time_step * 0.5 * (moved[0, 0:17] + moved[0, 1:18])
    x_self = frac_x * high(1)[:17]
    x_next = frac_x - x_self
    own = [moved[k, 1:17] for k in range(2)]
    y_sides = [shifts_y(own[k], rim[k]) for k in range(2)]
    frac_y = time_step * 0.5 * (own[1] + y_sides[1][0])
    frac_before = time_step * 0.5 * (own[1] + y_sides[1][1])
    flag = fields[2]
    flag_before = jnp.where(lane == 0, field_rim[2], pltpu.roll(flag, 1, 1))
    y_self, before_self = frac_y * flag, frac_before * flag_before
    y_next, before_next = frac_y - y_self, frac_before - before_self
    centre = 1.0 - x_self[1:17] + x_next[0:16] - y_self + before_next
    coefs = (centre, -x_next[1:17], x_self[0:16], -y_next, before_self)
    for k in range(2):
        velocity_out[k] = (
            centre * own[k]
            + coefs[1] * moved[k, 2:18]
            + coefs[2] * moved[k, 0:16]
            + coefs[3] * y_sides[k][0]
            + coefs[4] * y_sides[k][1]
        )
    return coefs


def remap_kernel(
    counts, velocity, fields, ux_even, ux_odd, uy_even, uy_odd, stress, sx_even, sx_odd, y_even, y_odd,
    relaxed_in, rows_even, rows_odd,
    out, velocity_out, relaxed, tall, moved, coefs, rows, cols, sems,
):
    block = pl.program_id(0)
    size = out.shape[1]
    gx, gy = places()
    odd_x = gx % 2 == 1

    def copy(i):
        part = pl.ds(i * size, size)
        return pltpu.make_async_copy(relaxed_in.at[:, part], relaxed.at[:, part], sems.at[i])

    @pl.when(block == 0)
    def _():
        for i in range(relaxed.shape[1] // size):
            copy(i).start()

    rows[0, :, :size] = jnp.where(odd_x, rows_odd[...], rows_even[...])
    rows[1, :, :size] = jnp.where(odd_x, rows_even[...], rows_odd[...])
    lane, row = lane_ids(16), row_ids()

    @pl.when(block == 0)
    def _():
        fresh = zone_update(
            counts,
            velocity,
            fields,
            (ux_even, ux_odd, uy_even, uy_odd),
            stress,
            (sx_even[...], sx_odd[...], y_even[48:72], y_odd[48:72]),
            tall,
            moved,
            velocity_out,
        )
        centre, east, west, north, south = fresh
        coefs[0] = centre
        coefs[1] = jnp.where(row == 15, 0.0, east)
        coefs[2] = jnp.where(row == 0, 0.0, west)
        coefs[3] = jnp.where(lane == 127, 0.0, north)
        coefs[4] = jnp.where(lane == 0, 0.0, south)
        coefs[5] = jnp.where((row == 15) & (gx < counts[0] - 1), east, 0.0)
        coefs[6] = jnp.where((row == 0) & (gx > 0), west, 0.0)
        rim = jnp.where((lane == 127) & (gy < counts[1] - 1), north, 0.0)
        coefs[7] = jnp.where((lane == 0) & (gy > 0), south, rim)
        odd_y = gy % 2 == 1
        for c in range(3):
            part = slice(16 * c, 16 * c + 16)
            got_even, got_odd = y_even[part], y_odd[part]
            after = jnp.where(odd_y, got_odd, got_even)
            before = jnp.where(odd_y, got_even, got_odd)
            cols[c] = jnp.where(lane % 2 == 0, after, pltpu.roll(before, 1, 1))
            cols[c + 3] = jnp.where(lane % 2 == 0, pltpu.roll(after, 127, 1), before)

    centre, east, west, north, south, _, _, rim = [coefs[i] for i in range(8)]
    high_east, low_west = coefs[5, 8:16], coefs[6, 0:8]
    copy(block).wait()

    def one(g):
        for c in range(6):
            q = relaxed[c, block * size + g]
            halo = pltpu.roll(cols[c], 127 - 2 * (block * size + g), 1)
            total = centre * q + north * pltpu.roll(q, 127, 1) + south * pltpu.roll(q, 1, 1)
            total = total + rim * halo
            total = total + east * pltpu.roll(q, 15, 0) + west * pltpu.roll(q, 1, 0)
            out[c, g, 0:8] = total[:8] + low_west * rows[1, c, pl.ds(g, 1), :]
            out[c, g, 8:16] = total[8:] + high_east * rows[0, c, pl.ds(g, 1), :]

    def some(i, carry):
        for k in range(16):
            one(i * 16 + k)
        return carry

    lax.fori_loop(0, size // 16, some, 0)


def remap_grains(velocity, fields, u_got, stress, s_got, y_got, relaxed, rows_even, rows_odd):
    n = relaxed.shape[1]
    size = 16
    small = (velocity, fields, *u_got, stress, *s_got, *y_got)
    return pl.pallas_call(
        functools.partial(remap_kernel, sizes()),
        grid=(n // size,),
        in_specs=[
            *[whole(*a.shape) for a in small],
            pl.BlockSpec(memory_space=pltpu.HBM),
            pl.BlockSpec((6, size, 128), lambda i: (0, i, 0)),
            pl.BlockSpec((6, size, 128), lambda i: (0, i, 0)),
        ],
        out_specs=[
            pl.BlockSpec((6, size, 16, 128), lambda i: (0, i, 0, 0)),
            whole(2, 16, 128),
        ],
        out_shape=[f32(*relaxed.shape), f32(2, 16, 128)],
        scratch_shapes=[
            pltpu.VMEM(relaxed.shape, jnp.float32),
            pltpu.VMEM((3, 32, 128), jnp.float32),
            pltpu.VMEM((2, 32, 128), jnp.float32),
            pltpu.VMEM((8, 16, 128), jnp.float32),
            pltpu.VMEM((2, 6, size + 8, 128), jnp.float32),
            pltpu.VMEM((6, 16, 128), jnp.float32),
            pltpu.SemaphoreType.DMA((n // size,)),
        ],
        compiler_params=pltpu.CompilerParams(vmem_limit_bytes=53 * 2**20),
        cost_estimate=pl.CostEstimate(flops=10**7, bytes_accessed=10**7, transcendentals=0),
    )(*small, relaxed, rows_even, rows_odd)


def swap_even(block, axis):
    return lax.ppermute(block, axis, [(i, i ^ 1) for i in range(lax.axis_size(axis))])


def swap_odd_y(block):
    count_x, count_y = sizes()
    pairs = []
    for x in range(count_x):
        for y in range(count_y):
            end = y in (0, count_y - 1)
            to_x, to_y = (x ^ 1, y) if end else (x, y + 1 if y % 2 else y - 1)
            pairs.append((x * count_y + y, to_x * count_y + to_y))
    return lax.ppermute(block, ("gx", "gy"), pairs)


def swap_odd_x(block, crossed):
    count = lax.axis_size("gx")
    pairs = []
    for x in range(count):
        for a in range(2):
            end = x in (0, count - 1)
            to_x = x if end else (x + 1 if x % 2 else x - 1)
            to_a = 1 - a if end or crossed else a
            pairs.append((x * 2 + a, to_x * 2 + to_a))
    return lax.ppermute(block, ("gx", "ga"), pairs)


def per_device(velocity, density, grain_stress, grain_angles, hardness, active, donor_faces):
    gx = lax.axis_index("gx")
    odd_x = gx % 2 == 1
    u_got = (
        swap_even(velocity, "gx"),
        swap_odd_x(velocity, True),
        swap_even(velocity, "gy"),
        swap_odd_y(velocity),
    )
    relaxed, part, rows_even, rows_odd, cols_even, cols_odd = solve_grains(
        0.5 * velocity, u_got, grain_stress, grain_angles, hardness, active
    )
    density, donor_faces, part = lax.optimization_barrier((density, donor_faces, part))
    fields = jnp.concatenate([(1.0 / density)[None], donor_faces.astype(jnp.float32)], axis=0)
    zone_stress = (part + swap_even(part, "ga")) * (1.0 / G)
    zone_stress, rows_even, rows_odd = lax.optimization_barrier((zone_stress, rows_even, rows_odd))
    far_rows_odd = swap_odd_x(rows_odd, False)
    far_rows_even = swap_even(rows_even, "gx")
    spare = jnp.zeros((7, 128), jnp.float32)
    first = jnp.concatenate([zone_stress[:, :2].reshape(6, 128), fields[:, 0], spare], axis=0)
    last = jnp.concatenate([zone_stress[:, -2:].reshape(6, 128), fields[:, -1], spare], axis=0)
    got_even = swap_even(jnp.where(odd_x, first, last), "gx")
    got_odd = swap_odd_x(jnp.where(odd_x, last, first), True)
    east, west = from_sides(got_even[:6], got_odd[:6], gx, lax.axis_size("gx"))
    east, west = east.reshape(3, 2, 128), west.reshape(3, 2, 128)
    tall = jnp.concatenate([west[:, 1:], zone_stress, east[:, :1]], axis=1)
    lane = lax.broadcasted_iota(jnp.int32, (18, 128), 1)
    sides = jnp.zeros((18, 128), jnp.float32)
    for c in range(3):
        sides = jnp.where(lane // 4 == c, jnp.roll(tall[c], 4 * c + 2, axis=1), sides)
    sides = jnp.pad(sides, ((0, 6), (0, 0)))
    lane = lax.broadcasted_iota(jnp.int32, (16, 128), 1)
    field_sides = jnp.zeros((16, 128), jnp.float32)
    for k in range(3):
        field_sides = jnp.where(lane // 2 == 6 + k, jnp.roll(fields[k], 13 + 2 * k, axis=1), field_sides)
    sides = sides + jnp.pad(field_sides, ((0, 8), (0, 0)))
    y_got = (
        swap_even(jnp.concatenate([cols_even.reshape(48, 128), sides], axis=0), "gy"),
        swap_odd_y(jnp.concatenate([cols_odd.reshape(48, 128), sides], axis=0)),
    )
    stress_out, velocity_out = remap_grains(
        velocity, fields, u_got, zone_stress, (got_even, got_odd), y_got, relaxed, far_rows_even, far_rows_odd
    )
    return (velocity_out, stress_out, zone_stress)


def solution(mesh):
    return jax.shard_map(
        per_device,
        mesh=mesh,
        in_specs=(
            P(None, "gx", "gy"),
            P("gx", "gy"),
            P(None, "ga", "gx", "gy"),
            P(None, "ga", "gx", "gy"),
            P("ga", "gx", "gy"),
            P(None, "ga", "gx", "gy"),
            P(None, "gx", "gy"),
        ),
        out_specs=(P(None, "gx", "gy"), P(None, "ga", "gx", "gy"), P(None, "gx", "gy")),
        check_vma=False,
    )
```

profile of v0, /device:TPU:120, one launch (start us, length us, event | category | flops | bytes accessed | tf_op | source)
XLA Modules:
  0.0 43.4 jit_solution(7043979445548575393)
XLA Ops:
  0.6 0.2 collective-permute-start.2
  0.8 2.4 %collective-permute-start.1 = (f32[2,16,128]{2,1,0:T(8,128)}, f32[2,16,128]{2,1,0:T(8,128)S(1)}, u32[]{:S(2)}, u32[]{:S(2)}) collective-permute-start(f32[2,16,128]{2,1,0:T(8,128)} %velocity.1), channel_id=1, source_target_pairs={{0,1},{1,0},{16,33},{17,32},{32,17},{33,16},{48,65},{49,64},{64,49... | collective-permute-start | bytes 49160 | tf_op jit(solution)/shard_map/ppermute | solution.py:604
  3.2 0.5 %collective-permute-start = (f32[2,16,128]{2,1,0:T(8,128)}, f32[2,16,128]{2,1,0:T(8,128)S(1)}, u32[]{:S(2)}, u32[]{:S(2)}) collective-permute-start(f32[2,16,128]{2,1,0:T(8,128)} %velocity.1), channel_id=1, source_target_pairs={{0,16},{16,0},{32,48},{48,32},{64,80},{80,64},{96,112},{112,96},{1... | collective-permute-start | bytes 49160 | tf_op jit(solution)/shard_map/ppermute | solution.py:581
  3.7 4.0 %collective-permute-start.3 = (f32[2,16,128]{2,1,0:T(8,128)}, f32[2,16,128]{2,1,0:T(8,128)S(1)}, u32[]{:S(2)}, u32[]{:S(2)}) collective-permute-start(f32[2,16,128]{2,1,0:T(8,128)} %velocity.1), channel_id=1, source_target_pairs={{0,16},{2,4},{4,2},{6,8},{8,6},{10,12},{12,10},{14,30},{16,0},{18,... | collective-permute-start | bytes 49160 | tf_op jit(solution)/shard_map/ppermute | solution.py:592
  7.8 0.7 %broadcast_multiply_fusion.half_velocity = f32[2,16,128]{2,1,0:T(8,128)S(1)} fusion(f32[2,16,128]{2,1,0:T(8,128)} %velocity.1), kind=kLoop, calls=%fused_computation.29 | loop fusion | flops 4096 | bytes 32768 | tf_op jit(solution)/shard_map/mul | solution.py:617
  8.5 0.1 pad.34.clone
  8.6 0.0 collective-permute-done.2.y_even.uy_even
  8.6 0.0 collective-permute-done.x_even.ux_even
  8.6 1.1 %collective-permute-done.3.y_odd.uy_odd = f32[2,16,128]{2,1,0:T(8,128)S(1)} collective-permute-done((f32[2,16,128]{2,1,0:T(8,128)}, f32[2,16,128]{2,1,0:T(8,128)S(1)}, u32[]{:S(2)}, u32[]{:S(2)}) %collective-permute-start.3) | collective-permute-done | bytes 16416 | tf_op jit(solution)/shard_map/ppermute | solution.py:592
  9.7 11.6 %shard_map.94 = (f32[6,64,16,128]{3,2,1,0:T(8,128)}, f32[3,16,128]{2,1,0:T(8,128)S(1)}, f32[6,64,128]{2,1,0:T(8,128)S(1)}, f32[6,64,128]{2,1,0:T(8,128)S(1)}, f3...) custom-call(f32[2,16,128]{2,1,0:T(8,128)S(1)} %broadcast_multiply_fusion.half_velocity, ...), custom_call_target="tpu_custom_call" | custom-call | flops 100000000 | bytes 10000000 | tf_op jit(solution)/shard_map/pallas_call | solution.py:366
  21.3 0.3 collective-permute-start.4
  21.6 0.1 slice.133
  21.7 0.1 slice.130
  21.8 0.1 slice.135
  21.8 3.4 %collective-permute-done.4 = f32[3,16,128]{2,1,0:T(8,128)S(1)} collective-permute-done((f32[3,16,128]{2,1,0:T(8,128)S(1)}, f32[3,16,128]{2,1,0:T(8,128)S(1)}, u32[]{:S(2)}, u32[]{:S(2)}) %collective-permute-start.4) | collective-permute-done | bytes 24608 | tf_op jit(solution)/shard_map/ppermute | solution.py:581
  25.3 0.1 fusion
  25.4 0.0 collective-permute-start.6
  25.4 0.1 collective-permute-start.5
  25.5 0.1 maximum_select_fusion.3
  25.6 0.5 %collective-permute-start.9 = (f32[6,64,128]{2,1,0:T(8,128)S(1)}, f32[6,64,128]{2,1,0:T(8,128)S(1)}, u32[]{:S(2)}, u32[]{:S(2)}) collective-permute-start(f32[6,64,128]{2,1,0:T(8,128)S(1)} %get-tuple-element.27), channel_id=1, source_target_pairs={{0,16},{16,0},{32,48},{48,32},{64,80},{80,64},{96,112},{112,96},{1... | collective-permute-start | bytes 589832 | tf_op jit(solution)/shard_map/ppermute | solution.py:581
  26.1 2.8 %collective-permute-start.10 = (f32[6,64,128]{2,1,0:T(8,128)S(1)}, f32[6,64,128]{2,1,0:T(8,128)S(1)}, u32[]{:S(2)}, u32[]{:S(2)}) collective-permute-start(f32[6,64,128]{2,1,0:T(8,128)S(1)} %get-tuple-element.28), channel_id=1, source_target_pairs={{0,1},{1,0},{16,32},{17,33},{32,16},{33,17},{48,64},{49,65},{64,48... | collective-permute-start | bytes 589832 | tf_op jit(solution)/shard_map/ppermute | solution.py:604
  28.9 1.7 %collective-permute-done.6.sx_odd = f32[16,128]{1,0:T(8,128)S(1)} collective-permute-done((f32[16,128]{1,0:T(8,128)S(1)}, f32[16,128]{1,0:T(8,128)S(1)}, u32[]{:S(2)}, u32[]{:S(2)}) %collective-permute-start.6) | collective-permute-done | bytes 8224 | tf_op jit(solution)/shard_map/ppermute | solution.py:604
  30.6 0.0 collective-permute-done.5.sx_even
  30.7 0.1 slice.127
  30.7 0.1 slice.124
  30.8 0.1 slice.121
  30.9 0.1 maximum_select_fusion
  31.0 3.3 %collective-permute-start.8 = (f32[72,128]{1,0:T(8,128)S(1)}, f32[72,128]{1,0:T(8,128)S(1)}, u32[]{:S(2)}, u32[]{:S(2)}) collective-permute-start(f32[72,128]{1,0:T(8,128)S(1)} %get-tuple-element.44), channel_id=1, source_target_pairs={{0,16},{2,4},{4,2},{6,8},{8,6},{10,12},{12,10},{14,30},{16,0},{18,... | collective-permute-start | bytes 110600 | tf_op jit(solution)/shard_map/ppermute | solution.py:592
  34.3 0.0 collective-permute-start.7
  34.3 1.9 %collective-permute-done.8.y_odd = f32[72,128]{1,0:T(8,128)S(1)} collective-permute-done((f32[72,128]{1,0:T(8,128)S(1)}, f32[72,128]{1,0:T(8,128)S(1)}, u32[]{:S(2)}, u32[]{:S(2)}) %collective-permute-start.8) | collective-permute-done | bytes 36896 | tf_op jit(solution)/shard_map/ppermute | solution.py:592
  36.2 2.0 %collective-permute-done.7.y_even = f32[72,128]{1,0:T(8,128)S(1)} collective-permute-done((f32[72,128]{1,0:T(8,128)S(1)}, f32[72,128]{1,0:T(8,128)S(1)}, u32[]{:S(2)}, u32[]{:S(2)}) %collective-permute-start.7) | collective-permute-done | bytes 36896 | tf_op jit(solution)/shard_map/ppermute | solution.py:581
  38.3 5.1 %shard_map.95 = (f32[6,64,16,128]{3,2,1,0:T(8,128)}, f32[2,16,128]{2,1,0:T(8,128)}) custom-call(f32[2,16,128]{2,1,0:T(8,128)S(1)} %copy-done.1, f32[3,16,128]{2,1,0:T(8,128)S(1)} %pad_maximum_fusion.2.fields, f32[2,16,128]{2,1,0:T(8,128)S(1)} %collective-permute-done.x_even.ux_even, f32[2,16,128]{2,1,0:T(8,128)S(1)} %collective-permute-done.1.x_odd.ux_odd, ...), custom_call_target="tpu_custom_call" | custom-call | flops 10000000 | bytes 10000000 | tf_op jit(solution)/shard_map/pallas_call | solution.py:552
  (35 shorter events, 0.2 us)
Async XLA Ops:
  0.6 8.0 %collective-permute-start.2 = (f32[2,16,128]{2,1,0:T(8,128)}, f32[2,16,128]{2,1,0:T(8,128)S(1)}, u32[]{:S(2)}, u32[]{:S(2)}) collective-permute-start(f32[2,16,128]{2,1,0:T(8,128)} %velocity.1), channel_id=1, source_target_pairs={{0,2},{2,0},{4,6},{6,4},{8,10},{10,8},{12,14},{14,12},{1,3},{3,1},... | collective-permute-start | bytes 49160 | tf_op jit(solution)/shard_map/ppermute | solution.py:581
  0.8 7.8 %collective-permute-start.1 = (f32[2,16,128]{2,1,0:T(8,128)}, f32[2,16,128]{2,1,0:T(8,128)S(1)}, u32[]{:S(2)}, u32[]{:S(2)}) collective-permute-start(f32[2,16,128]{2,1,0:T(8,128)} %velocity.1), channel_id=1, source_target_pairs={{0,1},{1,0},{16,33},{17,32},{32,17},{33,16},{48,65},{49,64},{64,49... | collective-permute-start | bytes 49160 | tf_op jit(solution)/shard_map/ppermute | solution.py:604
  3.2 5.4 %collective-permute-start = (f32[2,16,128]{2,1,0:T(8,128)}, f32[2,16,128]{2,1,0:T(8,128)S(1)}, u32[]{:S(2)}, u32[]{:S(2)}) collective-permute-start(f32[2,16,128]{2,1,0:T(8,128)} %velocity.1), channel_id=1, source_target_pairs={{0,16},{16,0},{32,48},{48,32},{64,80},{80,64},{96,112},{112,96},{1... | collective-permute-start | bytes 49160 | tf_op jit(solution)/shard_map/ppermute | solution.py:581
  3.7 6.0 %collective-permute-start.3 = (f32[2,16,128]{2,1,0:T(8,128)}, f32[2,16,128]{2,1,0:T(8,128)S(1)}, u32[]{:S(2)}, u32[]{:S(2)}) collective-permute-start(f32[2,16,128]{2,1,0:T(8,128)} %velocity.1), channel_id=1, source_target_pairs={{0,16},{2,4},{4,2},{6,8},{8,6},{10,12},{12,10},{14,30},{16,0},{18,... | collective-permute-start | bytes 49160 | tf_op jit(solution)/shard_map/ppermute | solution.py:592
  8.6 12.7 %copy-start.2 = (s32[2,16,128]{2,1,0:T(8,128)S(1)}, s32[2,16,128]{2,1,0:T(8,128)}, u32[]{:S(2)}) copy-start(s32[2,16,128]{2,1,0:T(8,128)} %param.13) | copy-start | bytes 49156
  8.6 12.7 %copy-start.3 = (f32[16,128]{1,0:T(8,128)S(1)}, f32[16,128]{1,0:T(8,128)}, u32[]{:S(2)}) copy-start(f32[16,128]{1,0:T(8,128)} %param.8) | copy-start | bytes 24580
  8.6 29.7 %copy-start.1 = (f32[2,16,128]{2,1,0:T(8,128)S(1)}, f32[2,16,128]{2,1,0:T(8,128)}, u32[]{:S(2)}) copy-start(f32[2,16,128]{2,1,0:T(8,128)} %velocity.1) | copy-start | bytes 49156
  21.3 3.9 %collective-permute-start.4 = (f32[3,16,128]{2,1,0:T(8,128)S(1)}, f32[3,16,128]{2,1,0:T(8,128)S(1)}, u32[]{:S(2)}, u32[]{:S(2)}) collective-permute-start(f32[3,16,128]{2,1,0:T(8,128)S(1)} %get-tuple-element.20), channel_id=1, source_target_pairs={{0,1},{1,0},{2,3},{3,2},{4,5},{5,4},{6,7},{7,6},{8,9},{9,8},{10,11... | collective-permute-start | bytes 73736 | tf_op jit(solution)/shard_map/ppermute | solution.py:581
  25.2 18.2 %copy-start = (f32[3,16,128]{2,1,0:T(8,128)}, f32[3,16,128]{2,1,0:T(8,128)S(1)}, u32[]{:S(2)}) copy-start(f32[3,16,128]{2,1,0:T(8,128)S(1)} %add_multiply_fusion.stress) | copy-start | bytes 73732
  25.4 5.2 %collective-permute-start.6 = (f32[16,128]{1,0:T(8,128)S(1)}, f32[16,128]{1,0:T(8,128)S(1)}, u32[]{:S(2)}, u32[]{:S(2)}) collective-permute-start(f32[16,128]{1,0:T(8,128)S(1)} %get-tuple-element.42), channel_id=1, source_target_pairs={{0,1},{1,0},{16,33},{17,32},{32,17},{33,16},{48,65},{49,64},{64,49... | collective-permute-start | bytes 24584 | tf_op jit(solution)/shard_map/ppermute | solution.py:604
  25.4 5.2 %collective-permute-start.5 = (f32[16,128]{1,0:T(8,128)S(1)}, f32[16,128]{1,0:T(8,128)S(1)}, u32[]{:S(2)}, u32[]{:S(2)}) collective-permute-start(f32[16,128]{1,0:T(8,128)S(1)} %get-tuple-element.43), channel_id=1, source_target_pairs={{0,16},{16,0},{32,48},{48,32},{64,80},{80,64},{96,112},{112,96},{1... | collective-permute-start | bytes 24584 | tf_op jit(solution)/shard_map/ppermute | solution.py:581
  25.6 12.7 %collective-permute-start.9 = (f32[6,64,128]{2,1,0:T(8,128)S(1)}, f32[6,64,128]{2,1,0:T(8,128)S(1)}, u32[]{:S(2)}, u32[]{:S(2)}) collective-permute-start(f32[6,64,128]{2,1,0:T(8,128)S(1)} %get-tuple-element.27), channel_id=1, source_target_pairs={{0,16},{16,0},{32,48},{48,32},{64,80},{80,64},{96,112},{112,96},{1... | collective-permute-start | bytes 589832 | tf_op jit(solution)/shard_map/ppermute | solution.py:581
  26.1 12.2 %collective-permute-start.10 = (f32[6,64,128]{2,1,0:T(8,128)S(1)}, f32[6,64,128]{2,1,0:T(8,128)S(1)}, u32[]{:S(2)}, u32[]{:S(2)}) collective-permute-start(f32[6,64,128]{2,1,0:T(8,128)S(1)} %get-tuple-element.28), channel_id=1, source_target_pairs={{0,1},{1,0},{16,32},{17,33},{32,16},{33,17},{48,64},{49,65},{64,48... | collective-permute-start | bytes 589832 | tf_op jit(solution)/shard_map/ppermute | solution.py:604
  31.0 5.3 %collective-permute-start.8 = (f32[72,128]{1,0:T(8,128)S(1)}, f32[72,128]{1,0:T(8,128)S(1)}, u32[]{:S(2)}, u32[]{:S(2)}) collective-permute-start(f32[72,128]{1,0:T(8,128)S(1)} %get-tuple-element.44), channel_id=1, source_target_pairs={{0,16},{2,4},{4,2},{6,8},{8,6},{10,12},{12,10},{14,30},{16,0},{18,... | collective-permute-start | bytes 110600 | tf_op jit(solution)/shard_map/ppermute | solution.py:592
  34.3 4.0 %collective-permute-start.7 = (f32[72,128]{1,0:T(8,128)S(1)}, f32[72,128]{1,0:T(8,128)S(1)}, u32[]{:S(2)}, u32[]{:S(2)}) collective-permute-start(f32[72,128]{1,0:T(8,128)S(1)} %get-tuple-element.45), channel_id=1, source_target_pairs={{0,2},{2,0},{4,6},{6,4},{8,10},{10,8},{12,14},{14,12},{1,3},{3,1},... | collective-permute-start | bytes 110600 | tf_op jit(solution)/shard_map/ppermute | solution.py:581
where the time goes:
time: 43.6 us; the launch traced here: 43.4 us
  Pallas kernels  16.7 us (38%)
  starting transfers between devices  14.2 us (33%)
  waiting for transfers between devices  10.1 us (23%)
  other arithmetic  1.05 us (2%)
  between operations  0.82 us (2%)
  local copies, waits for them, and re-layouts  0.59 us (1%)
    pallas_call x1, Pallas kernels, solve_grains(): pl.pallas_call(functools.partial(solve_kernel, sizes()), grid=(1,), in_sp...  11.6 us
    ppermute x2, starting transfers between devices, swap_odd_y(): return lax.ppermute(block, ('gx', 'gy'), pairs)  7.36 us
    ppermute x6, waiting for transfers between devices, swap_even(): lax.ppermute(block, axis, [(i, i ^ 1) for i in range(lax.axis_size(axis))])  5.41 us
    ppermute x3, starting transfers between devices, swap_odd_x(): return lax.ppermute(block, ('gx', 'ga'), pairs)  5.22 us
    pallas_call x1, Pallas kernels, remap_grains(): pl.pallas_call(functools.partial(remap_kernel, sizes()), grid=(n // size,...  5.15 us
    ppermute x2, waiting for transfers between devices, swap_odd_y(): return lax.ppermute(block, ('gx', 'gy'), pairs)  2.98 us
    ppermute x3, waiting for transfers between devices, swap_odd_x(): return lax.ppermute(block, ('gx', 'ga'), pairs)  1.66 us
    ppermute x6, starting transfers between devices, swap_even(): lax.ppermute(block, axis, [(i, i ^ 1) for i in range(lax.axis_size(axis))])  1.63 us
  transfers between devices with their start and end apart: 11, of which 5 were waited for; matrix products, arithmetic and copies ran while one was open for 3% of the time, Pallas kernels for 0%

commit v1 on v0

--- a/solution.py
+++ b/solution.py
@@ -469,7 +469,7 @@
 
 
 def remap_kernel(
-    counts, velocity, fields, ux_even, ux_odd, uy_even, uy_odd, stress, sx_even, sx_odd, y_even, y_odd,
+    counts, velocity, fields, ux_even, ux_odd, uy_even, uy_odd, stress, sx_even, sx_odd, y_odd, y_even,
     relaxed_in, rows_even, rows_odd,
     out, velocity_out, relaxed, tall, moved, coefs, rows, cols, sems,
 ):
@@ -640,10 +640,9 @@
     for k in range(3):
         field_sides = jnp.where(lane // 2 == 6 + k, jnp.roll(fields[k], 13 + 2 * k, axis=1), field_sides)
     sides = sides + jnp.pad(field_sides, ((0, 8), (0, 0)))
-    y_got = (
-        swap_even(jnp.concatenate([cols_even.reshape(48, 128), sides], axis=0), "gy"),
-        swap_odd_y(jnp.concatenate([cols_odd.reshape(48, 128), sides], axis=0)),
-    )
+    y_odd = swap_odd_y(jnp.concatenate([cols_odd.reshape(48, 128), sides], axis=0))
+    y_even = swap_even(jnp.concatenate([cols_even.reshape(48, 128), sides], axis=0), "gy")
+    y_got = (y_odd, y_even)
     stress_out, velocity_out = remap_grains(
         velocity, fields, u_got, zone_stress, (got_even, got_odd), y_got, relaxed, far_rows_even, far_rows_odd
     )

time: 43.6 us -> 42.3 us (0.970); the launches traced: 43.4 us -> 41.5 us
  waiting for transfers between devices: 10.1 us -> 8.04 us
    ppermute x6, waiting for transfers between devices: 5.41 us -> 4.01 us  [swap_even(): lax.ppermute(block, axis, [(i, i ^ 1) for i in range(lax.axis_size(axis))])]
    ppermute x2, waiting for transfers between devices: 2.98 us -> 2.37 us  [swap_odd_y(): return lax.ppermute(block, ('gx', 'gy'), pairs)]
  transfers between devices with their start and end apart: 11 -> 11, of which waited for: 5 -> 5; matrix products, arithmetic and copies ran while one was open for 3% -> 4% of each run, Pallas kernels for 0% -> 0%
where the time goes in v1:
time: 42.3 us; the launch traced here: 41.5 us
  Pallas kernels  16.7 us (39%)
  starting transfers between devices  14.3 us (34%)
  waiting for transfers between devices  8.04 us (19%)
  other arithmetic  1.05 us (2%)
  between operations  0.82 us (2%)
  local copies, waits for them, and re-layouts  0.59 us (1%)
    pallas_call x1, Pallas kernels, solve_grains(): pl.pallas_call(functools.partial(solve_kernel, sizes()), grid=(1,), in_sp...  11.6 us
    ppermute x2, starting transfers between devices, swap_odd_y(): return lax.ppermute(block, ('gx', 'gy'), pairs)  7.36 us
    ppermute x3, starting transfers between devices, swap_odd_x(): return lax.ppermute(block, ('gx', 'ga'), pairs)  5.22 us
    pallas_call x1, Pallas kernels, remap_grains(): pl.pallas_call(functools.partial(remap_kernel, sizes()), grid=(n // size,...  5.15 us
    ppermute x6, waiting for transfers between devices, swap_even(): lax.ppermute(block, axis, [(i, i ^ 1) for i in range(lax.axis_size(axis))])  4.01 us
    ppermute x2, waiting for transfers between devices, swap_odd_y(): return lax.ppermute(block, ('gx', 'gy'), pairs)  2.37 us
    ppermute x6, starting transfers between devices, swap_even(): lax.ppermute(block, axis, [(i, i ^ 1) for i in range(lax.axis_size(axis))])  1.72 us
    ppermute x3, waiting for transfers between devices, swap_odd_x(): return lax.ppermute(block, ('gx', 'ga'), pairs)  1.66 us
  transfers between devices with their start and end apart: 11, of which 5 were waited for; matrix products, arithmetic and copies ran while one was open for 4% of the time, Pallas kernels for 0%

profile of v1, /device:TPU:120, one launch (start us, length us, event | category | flops | bytes accessed | tf_op | source)
XLA Modules:
  0.0 41.5 jit_solution(7439110597147974382)
XLA Ops:
  0.6 0.2 collective-permute-start.2
  0.8 2.4 %collective-permute-start.1 = (f32[2,16,128]{2,1,0:T(8,128)}, f32[2,16,128]{2,1,0:T(8,128)S(1)}, u32[]{:S(2)}, u32[]{:S(2)}) collective-permute-start(f32[2,16,128]{2,1,0:T(8,128)} %velocity.1), channel_id=1, source_target_pairs={{0,1},{1,0},{16,33},{17,32},{32,17},{33,16},{48,65},{49,64},{64,49... | collective-permute-start | bytes 49160 | tf_op jit(solution)/shard_map/ppermute | solution.py:604
  3.2 0.5 %collective-permute-start = (f32[2,16,128]{2,1,0:T(8,128)}, f32[2,16,128]{2,1,0:T(8,128)S(1)}, u32[]{:S(2)}, u32[]{:S(2)}) collective-permute-start(f32[2,16,128]{2,1,0:T(8,128)} %velocity.1), channel_id=1, source_target_pairs={{0,16},{16,0},{32,48},{48,32},{64,80},{80,64},{96,112},{112,96},{1... | collective-permute-start | bytes 49160 | tf_op jit(solution)/shard_map/ppermute | solution.py:581
  3.7 4.0 %collective-permute-start.3 = (f32[2,16,128]{2,1,0:T(8,128)}, f32[2,16,128]{2,1,0:T(8,128)S(1)}, u32[]{:S(2)}, u32[]{:S(2)}) collective-permute-start(f32[2,16,128]{2,1,0:T(8,128)} %velocity.1), channel_id=1, source_target_pairs={{0,16},{2,4},{4,2},{6,8},{8,6},{10,12},{12,10},{14,30},{16,0},{18,... | collective-permute-start | bytes 49160 | tf_op jit(solution)/shard_map/ppermute | solution.py:592
  7.8 0.7 %broadcast_multiply_fusion.half_velocity = f32[2,16,128]{2,1,0:T(8,128)S(1)} fusion(f32[2,16,128]{2,1,0:T(8,128)} %velocity.1), kind=kLoop, calls=%fused_computation.29 | loop fusion | flops 4096 | bytes 32768 | tf_op jit(solution)/shard_map/mul | solution.py:617
  8.5 0.1 pad.34.clone
  8.6 0.0 collective-permute-done.1.x_odd.ux_odd
  8.6 0.0 collective-permute-done.x_even.ux_even
  8.6 1.1 %collective-permute-done.3.y_odd.uy_odd = f32[2,16,128]{2,1,0:T(8,128)S(1)} collective-permute-done((f32[2,16,128]{2,1,0:T(8,128)}, f32[2,16,128]{2,1,0:T(8,128)S(1)}, u32[]{:S(2)}, u32[]{:S(2)}) %collective-permute-start.3) | collective-permute-done | bytes 16416 | tf_op jit(solution)/shard_map/ppermute | solution.py:592
  9.7 11.6 %shard_map.94 = (f32[6,64,16,128]{3,2,1,0:T(8,128)}, f32[3,16,128]{2,1,0:T(8,128)S(1)}, f32[6,64,128]{2,1,0:T(8,128)S(1)}, f32[6,64,128]{2,1,0:T(8,128)S(1)}, f3...) custom-call(f32[2,16,128]{2,1,0:T(8,128)S(1)} %broadcast_multiply_fusion.half_velocity, ...), custom_call_target="tpu_custom_call" | custom-call | flops 100000000 | bytes 10000000 | tf_op jit(solution)/shard_map/pallas_call | solution.py:366
  21.3 0.3 collective-permute-start.4
  21.6 0.1 slice.133
  21.7 0.1 slice.130
  21.8 0.1 slice.135
  21.8 3.4 %collective-permute-done.4 = f32[3,16,128]{2,1,0:T(8,128)S(1)} collective-permute-done((f32[3,16,128]{2,1,0:T(8,128)S(1)}, f32[3,16,128]{2,1,0:T(8,128)S(1)}, u32[]{:S(2)}, u32[]{:S(2)}) %collective-permute-start.4) | collective-permute-done | bytes 24608 | tf_op jit(solution)/shard_map/ppermute | solution.py:581
  25.3 0.1 fusion
  25.4 0.0 collective-permute-start.6
  25.4 0.1 collective-permute-start.5
  25.5 0.1 maximum_select_fusion.3
  25.6 0.5 %collective-permute-start.9 = (f32[6,64,128]{2,1,0:T(8,128)S(1)}, f32[6,64,128]{2,1,0:T(8,128)S(1)}, u32[]{:S(2)}, u32[]{:S(2)}) collective-permute-start(f32[6,64,128]{2,1,0:T(8,128)S(1)} %get-tuple-element.27), channel_id=1, source_target_pairs={{0,16},{16,0},{32,48},{48,32},{64,80},{80,64},{96,112},{112,96},{1... | collective-permute-start | bytes 589832 | tf_op jit(solution)/shard_map/ppermute | solution.py:581
  26.1 2.8 %collective-permute-start.10 = (f32[6,64,128]{2,1,0:T(8,128)S(1)}, f32[6,64,128]{2,1,0:T(8,128)S(1)}, u32[]{:S(2)}, u32[]{:S(2)}) collective-permute-start(f32[6,64,128]{2,1,0:T(8,128)S(1)} %get-tuple-element.28), channel_id=1, source_target_pairs={{0,1},{1,0},{16,32},{17,33},{32,16},{33,17},{48,64},{49,65},{64,48... | collective-permute-start | bytes 589832 | tf_op jit(solution)/shard_map/ppermute | solution.py:604
  28.9 1.7 %collective-permute-done.6.sx_odd = f32[16,128]{1,0:T(8,128)S(1)} collective-permute-done((f32[16,128]{1,0:T(8,128)S(1)}, f32[16,128]{1,0:T(8,128)S(1)}, u32[]{:S(2)}, u32[]{:S(2)}) %collective-permute-start.6) | collective-permute-done | bytes 8224 | tf_op jit(solution)/shard_map/ppermute | solution.py:604
  30.6 0.0 collective-permute-done.5.sx_even
  30.7 0.1 slice.127
  30.7 0.1 slice.124
  30.8 0.1 slice.121
  30.9 0.1 maximum_select_fusion
  31.0 0.1 collective-permute-start.8
  31.1 3.3 %collective-permute-start.7 = (f32[72,128]{1,0:T(8,128)S(1)}, f32[72,128]{1,0:T(8,128)S(1)}, u32[]{:S(2)}, u32[]{:S(2)}) collective-permute-start(f32[72,128]{1,0:T(8,128)S(1)} %get-tuple-element.45), channel_id=1, source_target_pairs={{0,16},{2,4},{4,2},{6,8},{8,6},{10,12},{12,10},{14,30},{16,0},{18,... | collective-permute-start | bytes 110600 | tf_op jit(solution)/shard_map/ppermute | solution.py:592
  34.4 0.6 %collective-permute-done.8.y_even = f32[72,128]{1,0:T(8,128)S(1)} collective-permute-done((f32[72,128]{1,0:T(8,128)S(1)}, f32[72,128]{1,0:T(8,128)S(1)}, u32[]{:S(2)}, u32[]{:S(2)}) %collective-permute-start.8) | collective-permute-done | bytes 36896 | tf_op jit(solution)/shard_map/ppermute | solution.py:581
  35.0 1.3 %collective-permute-done.7.y_odd = f32[72,128]{1,0:T(8,128)S(1)} collective-permute-done((f32[72,128]{1,0:T(8,128)S(1)}, f32[72,128]{1,0:T(8,128)S(1)}, u32[]{:S(2)}, u32[]{:S(2)}) %collective-permute-start.7) | collective-permute-done | bytes 36896 | tf_op jit(solution)/shard_map/ppermute | solution.py:592
  36.4 5.1 %shard_map.95 = (f32[6,64,16,128]{3,2,1,0:T(8,128)}, f32[2,16,128]{2,1,0:T(8,128)}) custom-call(f32[2,16,128]{2,1,0:T(8,128)S(1)} %copy-done.1, f32[3,16,128]{2,1,0:T(8,128)S(1)} %pad_maximum_fusion.2.fields, f32[2,16,128]{2,1,0:T(8,128)S(1)} %collective-permute-done.x_even.ux_even, f32[2,16,128]{2,1,0:T(8,128)S(1)} %collective-permute-done.1.x_odd.ux_odd, ...), custom_call_target="tpu_custom_call" | custom-call | flops 10000000 | bytes 10000000 | tf_op jit(solution)/shard_map/pallas_call | solution.py:552
  (35 shorter events, 0.2 us)
Async XLA Ops:
  0.6 8.0 %collective-permute-start.2 = (f32[2,16,128]{2,1,0:T(8,128)}, f32[2,16,128]{2,1,0:T(8,128)S(1)}, u32[]{:S(2)}, u32[]{:S(2)}) collective-permute-start(f32[2,16,128]{2,1,0:T(8,128)} %velocity.1), channel_id=1, source_target_pairs={{0,2},{2,0},{4,6},{6,4},{8,10},{10,8},{12,14},{14,12},{1,3},{3,1},... | collective-permute-start | bytes 49160 | tf_op jit(solution)/shard_map/ppermute | solution.py:581
  0.8 7.8 %collective-permute-start.1 = (f32[2,16,128]{2,1,0:T(8,128)}, f32[2,16,128]{2,1,0:T(8,128)S(1)}, u32[]{:S(2)}, u32[]{:S(2)}) collective-permute-start(f32[2,16,128]{2,1,0:T(8,128)} %velocity.1), channel_id=1, source_target_pairs={{0,1},{1,0},{16,33},{17,32},{32,17},{33,16},{48,65},{49,64},{64,49... | collective-permute-start | bytes 49160 | tf_op jit(solution)/shard_map/ppermute | solution.py:604
  3.2 5.4 %collective-permute-start = (f32[2,16,128]{2,1,0:T(8,128)}, f32[2,16,128]{2,1,0:T(8,128)S(1)}, u32[]{:S(2)}, u32[]{:S(2)}) collective-permute-start(f32[2,16,128]{2,1,0:T(8,128)} %velocity.1), channel_id=1, source_target_pairs={{0,16},{16,0},{32,48},{48,32},{64,80},{80,64},{96,112},{112,96},{1... | collective-permute-start | bytes 49160 | tf_op jit(solution)/shard_map/ppermute | solution.py:581
  3.7 6.0 %collective-permute-start.3 = (f32[2,16,128]{2,1,0:T(8,128)}, f32[2,16,128]{2,1,0:T(8,128)S(1)}, u32[]{:S(2)}, u32[]{:S(2)}) collective-permute-start(f32[2,16,128]{2,1,0:T(8,128)} %velocity.1), channel_id=1, source_target_pairs={{0,16},{2,4},{4,2},{6,8},{8,6},{10,12},{12,10},{14,30},{16,0},{18,... | collective-permute-start | bytes 49160 | tf_op jit(solution)/shard_map/ppermute | solution.py:592
  8.6 12.7 %copy-start.2 = (s32[2,16,128]{2,1,0:T(8,128)S(1)}, s32[2,16,128]{2,1,0:T(8,128)}, u32[]{:S(2)}) copy-start(s32[2,16,128]{2,1,0:T(8,128)} %param.13) | copy-start | bytes 49156
  8.6 12.7 %copy-start.3 = (f32[16,128]{1,0:T(8,128)S(1)}, f32[16,128]{1,0:T(8,128)}, u32[]{:S(2)}) copy-start(f32[16,128]{1,0:T(8,128)} %param.8) | copy-start | bytes 24580
  8.6 27.8 %copy-start.1 = (f32[2,16,128]{2,1,0:T(8,128)S(1)}, f32[2,16,128]{2,1,0:T(8,128)}, u32[]{:S(2)}) copy-start(f32[2,16,128]{2,1,0:T(8,128)} %velocity.1) | copy-start | bytes 49156
  21.3 3.9 %collective-permute-start.4 = (f32[3,16,128]{2,1,0:T(8,128)S(1)}, f32[3,16,128]{2,1,0:T(8,128)S(1)}, u32[]{:S(2)}, u32[]{:S(2)}) collective-permute-start(f32[3,16,128]{2,1,0:T(8,128)S(1)} %get-tuple-element.20), channel_id=1, source_target_pairs={{0,1},{1,0},{2,3},{3,2},{4,5},{5,4},{6,7},{7,6},{8,9},{9,8},{10,11... | collective-permute-start | bytes 73736 | tf_op jit(solution)/shard_map/ppermute | solution.py:581
  25.2 16.3 %copy-start = (f32[3,16,128]{2,1,0:T(8,128)}, f32[3,16,128]{2,1,0:T(8,128)S(1)}, u32[]{:S(2)}) copy-start(f32[3,16,128]{2,1,0:T(8,128)S(1)} %add_multiply_fusion.stress) | copy-start | bytes 73732
  25.4 5.2 %collective-permute-start.6 = (f32[16,128]{1,0:T(8,128)S(1)}, f32[16,128]{1,0:T(8,128)S(1)}, u32[]{:S(2)}, u32[]{:S(2)}) collective-permute-start(f32[16,128]{1,0:T(8,128)S(1)} %get-tuple-element.42), channel_id=1, source_target_pairs={{0,1},{1,0},{16,33},{17,32},{32,17},{33,16},{48,65},{49,64},{64,49... | collective-permute-start | bytes 24584 | tf_op jit(solution)/shard_map/ppermute | solution.py:604
  25.4 5.2 %collective-permute-start.5 = (f32[16,128]{1,0:T(8,128)S(1)}, f32[16,128]{1,0:T(8,128)S(1)}, u32[]{:S(2)}, u32[]{:S(2)}) collective-permute-start(f32[16,128]{1,0:T(8,128)S(1)} %get-tuple-element.43), channel_id=1, source_target_pairs={{0,16},{16,0},{32,48},{48,32},{64,80},{80,64},{96,112},{112,96},{1... | collective-permute-start | bytes 24584 | tf_op jit(solution)/shard_map/ppermute | solution.py:581
  25.6 10.8 %collective-permute-start.9 = (f32[6,64,128]{2,1,0:T(8,128)S(1)}, f32[6,64,128]{2,1,0:T(8,128)S(1)}, u32[]{:S(2)}, u32[]{:S(2)}) collective-permute-start(f32[6,64,128]{2,1,0:T(8,128)S(1)} %get-tuple-element.27), channel_id=1, source_target_pairs={{0,16},{16,0},{32,48},{48,32},{64,80},{80,64},{96,112},{112,96},{1... | collective-permute-start | bytes 589832 | tf_op jit(solution)/shard_map/ppermute | solution.py:581
  26.1 10.3 %collective-permute-start.10 = (f32[6,64,128]{2,1,0:T(8,128)S(1)}, f32[6,64,128]{2,1,0:T(8,128)S(1)}, u32[]{:S(2)}, u32[]{:S(2)}) collective-permute-start(f32[6,64,128]{2,1,0:T(8,128)S(1)} %get-tuple-element.28), channel_id=1, source_target_pairs={{0,1},{1,0},{16,32},{17,33},{32,16},{33,17},{48,64},{49,65},{64,48... | collective-permute-start | bytes 589832 | tf_op jit(solution)/shard_map/ppermute | solution.py:604
  31.0 4.0 %collective-permute-start.8 = (f32[72,128]{1,0:T(8,128)S(1)}, f32[72,128]{1,0:T(8,128)S(1)}, u32[]{:S(2)}, u32[]{:S(2)}) collective-permute-start(f32[72,128]{1,0:T(8,128)S(1)} %get-tuple-element.44), channel_id=1, source_target_pairs={{0,2},{2,0},{4,6},{6,4},{8,10},{10,8},{12,14},{14,12},{1,3},{3,1},... | collective-permute-start | bytes 110600 | tf_op jit(solution)/shard_map/ppermute | solution.py:581
  31.1 5.3 %collective-permute-start.7 = (f32[72,128]{1,0:T(8,128)S(1)}, f32[72,128]{1,0:T(8,128)S(1)}, u32[]{:S(2)}, u32[]{:S(2)}) collective-permute-start(f32[72,128]{1,0:T(8,128)S(1)} %get-tuple-element.45), channel_id=1, source_target_pairs={{0,16},{2,4},{4,2},{6,8},{8,6},{10,12},{12,10},{14,30},{16,0},{18,... | collective-permute-start | bytes 110600 | tf_op jit(solution)/shard_map/ppermute | solution.py:592
